TPU v7x, 32 devices: a whole 2x2x4 slice. The times are simulated.
32 devices in a mesh: tm: 16 (over z, x, core), space: 2 (over y).
Axes of the slice: x: 2, y: 2, z: 4, core: 2. Of those that a mesh axis runs over, the one named last changes fastest.
Arguments:
- rhs: float32 [16, 3, 128, 256], P('tm', None, 'space'), may hold values from -6 to 6
- depth: float32 [128, 256], P('space'), may hold values from 0.25 to 2
- coriolis: float32 [128, 256], P('space'), may hold values from -0.05 to 0.05
Outputs:
- preconditioned: float32 [16, 3, 128, 256], P('tm', None, 'space')
All inputs are finite; a program needn't handle non-finite values.
Results may differ from a plain program's by a relative error of at most 0.0003.
Values sent between devices are 32-bit elements; how exact they have to be, the bound alone decides.
A program may use at most 64 MiB of HBM per device.

v0:
```python
import math

import jax
import jax.numpy as jnp
from jax import lax
from jax.sharding import PartitionSpec as P

SWEEPS = 8


RHO = 0.9
SIGMA = 0.01


def partner_2(x, axis, stride):
    return lax.ppermute(x, axis, [(i, i ^ 1 << stride) for i in range(lax.axis_size(axis))])


def extended(x, sides, width):
    for axis, dim in sides:
        devices, length = (lax.axis_size(axis), x.shape[dim])
        up = [(i, (i + 1) % devices) for i in range(devices - 1)]
        down = [(j, i) for i, j in up]
        last = lax.slice_in_dim(x, length - width, length, axis=dim)
        initial = lax.slice_in_dim(x, 0, width, axis=dim)
        before = lax.ppermute(last, axis, up)
        after = lax.ppermute(initial, axis, down)
        x = jnp.concatenate([before, x, after], axis=dim)
    return x


def tendency(height, east, north, height_ext, east_ext, depth, coriolis):
    height_dx = height_ext[2:] - height_ext[:-2]
    east_dx = east_ext[2:] - east_ext[:-2]
    height_dy = jnp.roll(height, -1, axis=1) - jnp.roll(height, 1, axis=1)
    north_dy = jnp.roll(north, -1, axis=1) - jnp.roll(north, 1, axis=1)
    return jnp.stack(
        [
            -SIGMA * depth * (east_dx + north_dy),
            -SIGMA * height_dx + coriolis * north,
            -SIGMA * height_dy - coriolis * east,
        ]
    )


def divide(real_part, imag_part, shift_re, shift_im):
    denom = shift_re * shift_re + shift_im * shift_im
    return (
        (real_part * shift_re + imag_part * shift_im) / denom,
        (imag_part * shift_re - real_part * shift_im) / denom,
    )


def pairs_forward(scaled, position, levels):
    real_part = scaled
    imag_part = jnp.zeros_like(scaled)
    frequency = jnp.zeros((), jnp.int32)
    for level in reversed(range(levels)):
        span = 1 << level
        packed = jnp.stack([real_part, imag_part])
        partner = partner_2(packed, "tm", level)
        upper_bit = position // span % 2
        upper = upper_bit == 1
        angle = -math.pi * (position % span).astype(jnp.float32) / span
        twid_re = jnp.cos(angle)
        twid_im = jnp.sin(angle)
        diff_re = partner[0] - real_part
        diff_im = partner[1] - imag_part
        new_re = jnp.where(upper, diff_re * twid_re - diff_im * twid_im, real_part + partner[0])
        new_im = jnp.where(upper, diff_re * twid_im + diff_im * twid_re, imag_part + partner[1])
        real_part, imag_part = (new_re, new_im)
        frequency = frequency + upper_bit * (1 << levels - 1 - level)
    return (real_part, imag_part, frequency)


def pairs_inverse(real_part, imag_part, position, levels, window):
    for level in range(levels):
        span = 1 << level
        packed = jnp.stack([real_part, imag_part])
        partner = partner_2(packed, "tm", level)
        upper = position // span % 2 == 1
        angle = math.pi * (position % span).astype(jnp.float32) / span
        twid_re = jnp.cos(angle)
        twid_im = jnp.sin(angle)
        turned_re = partner[0] * twid_re - partner[1] * twid_im
        turned_im = partner[0] * twid_im + partner[1] * twid_re
        mine_re = real_part * twid_re - imag_part * twid_im
        mine_im = real_part * twid_im + imag_part * twid_re
        new_re = jnp.where(upper, partner[0] - mine_re, real_part + turned_re)
        new_im = jnp.where(upper, partner[1] - mine_im, imag_part + turned_im)
        real_part, imag_part = (new_re, new_im)
    return real_part / window


def solve_single(right_re, right_im, shift_re, shift_im, depth, coriolis):
    work_re, work_im = divide(right_re, right_im, shift_re, shift_im)
    for sweep in range(SWEEPS):
        packed = jnp.stack([work_re[0], work_re[1], work_im[0], work_im[1]])
        padded = extended(packed, (("space", 1),), 1)
        moved_re = tendency(
            work_re[0], work_re[1], work_re[2], padded[0], padded[1], depth, coriolis
        )
        moved_im = tendency(
            work_im[0], work_im[1], work_im[2], padded[2], padded[3], depth, coriolis
        )
        work_re, work_im = divide(right_re + moved_re, right_im + moved_im, shift_re, shift_im)
    return (work_re, work_im)


def shards(rhs, depth, coriolis):
    window = lax.axis_size("tm")
    levels = window.bit_length() - 1
    position = lax.axis_index("tm")
    moment = position.astype(jnp.float32)
    scaled = rhs[0] * jnp.power(jnp.float32(RHO), moment)
    spec_re, spec_im, frequency = pairs_forward(scaled, position, levels)
    theta = 2.0 * math.pi * frequency.astype(jnp.float32) / window
    shift_re = 1.0 - RHO * jnp.cos(theta)
    shift_im = RHO * jnp.sin(theta)
    solved_re, solved_im = solve_single(spec_re, spec_im, shift_re, shift_im, depth, coriolis)
    result = pairs_inverse(solved_re, solved_im, position, levels, window)
    return (result * jnp.power(jnp.float32(RHO), -moment))[None]


def solution(mesh):
    in_specs = (P("tm", None, "space", None), P("space", None), P("space", None))
    out_specs = P("tm", None, "space", None)
    return jax.shard_map(shards, mesh=mesh, in_specs=in_specs, out_specs=out_specs, check_vma=False)
```

profile of v0, /device:TPU:0, one launch (start us, length us, event | category | flops | bytes accessed | tf_op | source)
XLA Modules:
  0.0 156.7 jit_solution(1637412523076395837)
XLA Ops:
  1.0 4.1 %collective-permute-start = (f32[2,3,64,256]{3,2,1,0:T(8,128)S(1)}, f32[2,3,64,256]{3,2,1,0:T(8,128)S(1)}, u32[]{:S(2)}, u32[]{:S(2)}) collective-permute-start(f32[2,3,64,256]{3,2,1,0:T(8,128)S(1)} %stack.263), channel_id=1, source_target_pairs={{0,16},{2,18},{4,20},{6,22},{8,24},{10,26},{12,28},{14,30},{16,0},... | collective-permute-start | bytes 1179656 | tf_op jit(solution)/shard_map/ppermute | solution.py:16
  5.3 17.4 %collective-permute-done = f32[2,3,64,256]{3,2,1,0:T(8,128)S(1)} collective-permute-done((f32[2,3,64,256]{3,2,1,0:T(8,128)S(1)}, f32[2,3,64,256]{3,2,1,0:T(8,128)S(1)}, u32[]{:S(2)}, u32[]{:S(2)}) %collective-permute-start) | collective-permute-done | bytes 393248 | tf_op jit(solution)/shard_map/ppermute | solution.py:16
  23.8 9.4 %collective-permute-done.1 = f32[2,3,64,256]{3,2,1,0:T(8,128)S(1)} collective-permute-done((f32[2,3,64,256]{3,2,1,0:T(8,128)S(1)}, f32[2,3,64,256]{3,2,1,0:T(8,128)S(1)}, u32[]{:S(2)}, u32[]{:S(2)}) %collective-permute-start.1) | collective-permute-done | bytes 393248 | tf_op jit(solution)/shard_map/ppermute | solution.py:16
  34.8 8.0 %collective-permute-done.2 = f32[2,3,64,256]{3,2,1,0:T(8,128)S(1)} collective-permute-done((f32[2,3,64,256]{3,2,1,0:T(8,128)S(1)}, f32[2,3,64,256]{3,2,1,0:T(8,128)S(1)}, u32[]{:S(2)}, u32[]{:S(2)}) %collective-permute-start.2) | collective-permute-done | bytes 393248 | tf_op jit(solution)/shard_map/ppermute | solution.py:16
  45.3 3.2 %collective-permute-start.5 = (f32[4,1,256]{2,1,0:T(1,128)S(1)}, f32[4,1,256]{2,1,0:T(1,128)S(1)}, u32[]{:S(2)}, u32[]{:S(2)}) collective-permute-start(f32[4,1,256]{2,1,0:T(1,128)S(1)} %get-tuple-element.71), channel_id=1, source_target_pairs={{0,1},{2,3},{4,5},{6,7},{8,9},{10,11},{12,13},{14,15},{16,17},{18,... | collective-permute-start | bytes 12296 | tf_op jit(solution)/shard_map/ppermute | solution.py:26
  50.9 3.2 %collective-permute-done.4 = f32[4,1,256]{2,1,0:T(1,128)S(1)} collective-permute-done((f32[4,1,256]{2,1,0:T(1,128)S(1)}, f32[4,1,256]{2,1,0:T(1,128)S(1)}, u32[]{:S(2)}, u32[]{:S(2)}) %collective-permute-start.4) | collective-permute-done | bytes 4128 | tf_op jit(solution)/shard_map/ppermute | solution.py:27
  54.9 2.2 %collective-permute-start.7 = (f32[4,1,256]{2,1,0:T(1,128)S(1)}, f32[4,1,256]{2,1,0:T(1,128)S(1)}, u32[]{:S(2)}, u32[]{:S(2)}) collective-permute-start(f32[4,1,256]{2,1,0:T(1,128)S(1)} %get-tuple-element.69), channel_id=1, source_target_pairs={{0,1},{2,3},{4,5},{6,7},{8,9},{10,11},{12,13},{14,15},{16,17},{18,... | collective-permute-start | bytes 12296 | tf_op jit(solution)/shard_map/ppermute | solution.py:26
  58.7 3.9 %collective-permute-done.6 = f32[4,1,256]{2,1,0:T(1,128)S(1)} collective-permute-done((f32[4,1,256]{2,1,0:T(1,128)S(1)}, f32[4,1,256]{2,1,0:T(1,128)S(1)}, u32[]{:S(2)}, u32[]{:S(2)}) %collective-permute-start.6) | collective-permute-done | bytes 4128 | tf_op jit(solution)/shard_map/ppermute | solution.py:27
  63.5 1.7 %collective-permute-start.9 = (f32[4,1,256]{2,1,0:T(1,128)S(1)}, f32[4,1,256]{2,1,0:T(1,128)S(1)}, u32[]{:S(2)}, u32[]{:S(2)}) collective-permute-start(f32[4,1,256]{2,1,0:T(1,128)S(1)} %get-tuple-element.67), channel_id=1, source_target_pairs={{0,1},{2,3},{4,5},{6,7},{8,9},{10,11},{12,13},{14,15},{16,17},{18,... | collective-permute-start | bytes 12296 | tf_op jit(solution)/shard_map/ppermute | solution.py:26
  66.8 3.9 %collective-permute-done.8 = f32[4,1,256]{2,1,0:T(1,128)S(1)} collective-permute-done((f32[4,1,256]{2,1,0:T(1,128)S(1)}, f32[4,1,256]{2,1,0:T(1,128)S(1)}, u32[]{:S(2)}, u32[]{:S(2)}) %collective-permute-start.8) | collective-permute-done | bytes 4128 | tf_op jit(solution)/shard_map/ppermute | solution.py:27
  71.6 1.7 %collective-permute-start.11 = (f32[4,1,256]{2,1,0:T(1,128)S(1)}, f32[4,1,256]{2,1,0:T(1,128)S(1)}, u32[]{:S(2)}, u32[]{:S(2)}) collective-permute-start(f32[4,1,256]{2,1,0:T(1,128)S(1)} %get-tuple-element.65), channel_id=1, source_target_pairs={{0,1},{2,3},{4,5},{6,7},{8,9},{10,11},{12,13},{14,15},{16,17},{18,... | collective-permute-start | bytes 12296 | tf_op jit(solution)/shard_map/ppermute | solution.py:26
  74.8 3.9 %collective-permute-done.10 = f32[4,1,256]{2,1,0:T(1,128)S(1)} collective-permute-done((f32[4,1,256]{2,1,0:T(1,128)S(1)}, f32[4,1,256]{2,1,0:T(1,128)S(1)}, u32[]{:S(2)}, u32[]{:S(2)}) %collective-permute-start.10) | collective-permute-done | bytes 4128 | tf_op jit(solution)/shard_map/ppermute | solution.py:27
  82.9 3.9 %collective-permute-done.12 = f32[4,1,256]{2,1,0:T(1,128)S(1)} collective-permute-done((f32[4,1,256]{2,1,0:T(1,128)S(1)}, f32[4,1,256]{2,1,0:T(1,128)S(1)}, u32[]{:S(2)}, u32[]{:S(2)}) %collective-permute-start.12) | collective-permute-done | bytes 4128 | tf_op jit(solution)/shard_map/ppermute | solution.py:27
  87.7 1.7 %collective-permute-start.15 = (f32[4,1,256]{2,1,0:T(1,128)S(1)}, f32[4,1,256]{2,1,0:T(1,128)S(1)}, u32[]{:S(2)}, u32[]{:S(2)}) collective-permute-start(f32[4,1,256]{2,1,0:T(1,128)S(1)} %get-tuple-element.61), channel_id=1, source_target_pairs={{0,1},{2,3},{4,5},{6,7},{8,9},{10,11},{12,13},{14,15},{16,17},{18,... | collective-permute-start | bytes 12296 | tf_op jit(solution)/shard_map/ppermute | solution.py:26
  91.0 3.9 %collective-permute-done.14 = f32[4,1,256]{2,1,0:T(1,128)S(1)} collective-permute-done((f32[4,1,256]{2,1,0:T(1,128)S(1)}, f32[4,1,256]{2,1,0:T(1,128)S(1)}, u32[]{:S(2)}, u32[]{:S(2)}) %collective-permute-start.14) | collective-permute-done | bytes 4128 | tf_op jit(solution)/shard_map/ppermute | solution.py:27
  95.8 1.7 %collective-permute-start.17 = (f32[4,1,256]{2,1,0:T(1,128)S(1)}, f32[4,1,256]{2,1,0:T(1,128)S(1)}, u32[]{:S(2)}, u32[]{:S(2)}) collective-permute-start(f32[4,1,256]{2,1,0:T(1,128)S(1)} %get-tuple-element.59), channel_id=1, source_target_pairs={{0,1},{2,3},{4,5},{6,7},{8,9},{10,11},{12,13},{14,15},{16,17},{18,... | collective-permute-start | bytes 12296 | tf_op jit(solution)/shard_map/ppermute | solution.py:26
  99.0 3.9 %collective-permute-done.16 = f32[4,1,256]{2,1,0:T(1,128)S(1)} collective-permute-done((f32[4,1,256]{2,1,0:T(1,128)S(1)}, f32[4,1,256]{2,1,0:T(1,128)S(1)}, u32[]{:S(2)}, u32[]{:S(2)}) %collective-permute-start.16) | collective-permute-done | bytes 4128 | tf_op jit(solution)/shard_map/ppermute | solution.py:27
  107.1 3.9 %collective-permute-done.18 = f32[4,1,256]{2,1,0:T(1,128)S(1)} collective-permute-done((f32[4,1,256]{2,1,0:T(1,128)S(1)}, f32[4,1,256]{2,1,0:T(1,128)S(1)}, u32[]{:S(2)}, u32[]{:S(2)}) %collective-permute-start.18) | collective-permute-done | bytes 4128 | tf_op jit(solution)/shard_map/ppermute | solution.py:27
  111.5 1.7 %collective-permute-done.20 = f32[2,3,64,256]{3,2,1,0:T(8,128)S(1)} collective-permute-done((f32[2,3,64,256]{3,2,1,0:T(8,128)S(1)}, f32[2,3,64,256]{3,2,1,0:T(8,128)S(1)}, u32[]{:S(2)}, u32[]{:S(2)}) %collective-permute-start.20) | collective-permute-done | bytes 393248 | tf_op jit(solution)/shard_map/ppermute | solution.py:16
  115.1 9.5 %collective-permute-done.21 = f32[2,3,64,256]{3,2,1,0:T(8,128)S(1)} collective-permute-done((f32[2,3,64,256]{3,2,1,0:T(8,128)S(1)}, f32[2,3,64,256]{3,2,1,0:T(8,128)S(1)}, u32[]{:S(2)}, u32[]{:S(2)}) %collective-permute-start.21) | collective-permute-done | bytes 393248 | tf_op jit(solution)/shard_map/ppermute | solution.py:16
  124.8 2.5 %collective-permute-start.22 = (f32[2,3,64,256]{3,2,1,0:T(8,128)S(1)}, f32[2,3,64,256]{3,2,1,0:T(8,128)S(1)}, u32[]{:S(2)}, u32[]{:S(2)}) collective-permute-start(f32[2,3,64,256]{3,2,1,0:T(8,128)S(1)} %pad_maximum_fusion.5), channel_id=1, source_target_pairs={{0,8},{2,10},{4,12},{6,14},{8,0},{10,2},{12,4},{14,6},{16,24},{18,... | collective-permute-start | bytes 1179656 | tf_op jit(solution)/shard_map/ppermute | solution.py:16
  127.5 8.4 %collective-permute-done.22 = f32[2,3,64,256]{3,2,1,0:T(8,128)S(1)} collective-permute-done((f32[2,3,64,256]{3,2,1,0:T(8,128)S(1)}, f32[2,3,64,256]{3,2,1,0:T(8,128)S(1)}, u32[]{:S(2)}, u32[]{:S(2)}) %collective-permute-start.22) | collective-permute-done | bytes 393248 | tf_op jit(solution)/shard_map/ppermute | solution.py:16
  136.1 3.8 %collective-permute-start.23 = (f32[2,3,64,256]{3,2,1,0:T(8,128)S(1)}, f32[2,3,64,256]{3,2,1,0:T(8,128)S(1)}, u32[]{:S(2)}, u32[]{:S(2)}) collective-permute-start(f32[2,3,64,256]{3,2,1,0:T(8,128)S(1)} %pad_maximum_fusion.6), channel_id=1, source_target_pairs={{0,16},{2,18},{4,20},{6,22},{8,24},{10,26},{12,28},{14,30},{16,0},... | collective-permute-start | bytes 1179656 | tf_op jit(solution)/shard_map/ppermute | solution.py:16
  140.0 15.9 %collective-permute-done.23 = f32[2,3,64,256]{3,2,1,0:T(8,128)S(1)} collective-permute-done((f32[2,3,64,256]{3,2,1,0:T(8,128)S(1)}, f32[2,3,64,256]{3,2,1,0:T(8,128)S(1)}, u32[]{:S(2)}, u32[]{:S(2)}) %collective-permute-start.23) | collective-permute-done | bytes 393248 | tf_op jit(solution)/shard_map/ppermute | solution.py:16
  (192 shorter events, 31.4 us)
Async XLA Ops:
  1.0 21.6 %collective-permute-start = (f32[2,3,64,256]{3,2,1,0:T(8,128)S(1)}, f32[2,3,64,256]{3,2,1,0:T(8,128)S(1)}, u32[]{:S(2)}, u32[]{:S(2)}) collective-permute-start(f32[2,3,64,256]{3,2,1,0:T(8,128)S(1)} %stack.263), channel_id=1, source_target_pairs={{0,16},{2,18},{4,20},{6,22},{8,24},{10,26},{12,28},{14,30},{16,0},... | collective-permute-start | bytes 1179656 | tf_op jit(solution)/shard_map/ppermute | solution.py:16
  22.8 10.4 %collective-permute-start.1 = (f32[2,3,64,256]{3,2,1,0:T(8,128)S(1)}, f32[2,3,64,256]{3,2,1,0:T(8,128)S(1)}, u32[]{:S(2)}, u32[]{:S(2)}) collective-permute-start(f32[2,3,64,256]{3,2,1,0:T(8,128)S(1)} %pad_maximum_fusion), channel_id=1, source_target_pairs={{0,8},{2,10},{4,12},{6,14},{8,0},{10,2},{12,4},{14,6},{16,24},{18,... | collective-permute-start | bytes 1179656 | tf_op jit(solution)/shard_map/ppermute | solution.py:16
  33.3 9.4 %collective-permute-start.2 = (f32[2,3,64,256]{3,2,1,0:T(8,128)S(1)}, f32[2,3,64,256]{3,2,1,0:T(8,128)S(1)}, u32[]{:S(2)}, u32[]{:S(2)}) collective-permute-start(f32[2,3,64,256]{3,2,1,0:T(8,128)S(1)} %pad_maximum_fusion.1), channel_id=1, source_target_pairs={{0,4},{2,6},{4,0},{6,2},{8,12},{10,14},{12,8},{14,10},{16,20},{18,... | collective-permute-start | bytes 1179656 | tf_op jit(solution)/shard_map/ppermute | solution.py:16
  42.9 1.8 %collective-permute-start.3 = (f32[2,3,64,256]{3,2,1,0:T(8,128)S(1)}, f32[2,3,64,256]{3,2,1,0:T(8,128)S(1)}, u32[]{:S(2)}, u32[]{:S(2)}) collective-permute-start(f32[2,3,64,256]{3,2,1,0:T(8,128)S(1)} %pad_maximum_fusion.2), channel_id=1, source_target_pairs={{0,2},{2,0},{4,6},{6,4},{8,10},{10,8},{12,14},{14,12},{16,18},{18,... | collective-permute-start | bytes 1179656 | tf_op jit(solution)/shard_map/ppermute | solution.py:16
  45.3 5.6 %collective-permute-start.5 = (f32[4,1,256]{2,1,0:T(1,128)S(1)}, f32[4,1,256]{2,1,0:T(1,128)S(1)}, u32[]{:S(2)}, u32[]{:S(2)}) collective-permute-start(f32[4,1,256]{2,1,0:T(1,128)S(1)} %get-tuple-element.71), channel_id=1, source_target_pairs={{0,1},{2,3},{4,5},{6,7},{8,9},{10,11},{12,13},{14,15},{16,17},{18,... | collective-permute-start | bytes 12296 | tf_op jit(solution)/shard_map/ppermute | solution.py:26
  48.5 5.5 %collective-permute-start.4 = (f32[4,1,256]{2,1,0:T(1,128)S(1)}, f32[4,1,256]{2,1,0:T(1,128)S(1)}, u32[]{:S(2)}, u32[]{:S(2)}) collective-permute-start(f32[4,1,256]{2,1,0:T(1,128)S(1)} %get-tuple-element.70), channel_id=1, source_target_pairs={{1,0},{3,2},{5,4},{7,6},{9,8},{11,10},{13,12},{15,14},{17,16},{19,... | collective-permute-start | bytes 12296 | tf_op jit(solution)/shard_map/ppermute | solution.py:27
  54.9 3.8 %collective-permute-start.7 = (f32[4,1,256]{2,1,0:T(1,128)S(1)}, f32[4,1,256]{2,1,0:T(1,128)S(1)}, u32[]{:S(2)}, u32[]{:S(2)}) collective-permute-start(f32[4,1,256]{2,1,0:T(1,128)S(1)} %get-tuple-element.69), channel_id=1, source_target_pairs={{0,1},{2,3},{4,5},{6,7},{8,9},{10,11},{12,13},{14,15},{16,17},{18,... | collective-permute-start | bytes 12296 | tf_op jit(solution)/shard_map/ppermute | solution.py:26
  57.1 5.5 %collective-permute-start.6 = (f32[4,1,256]{2,1,0:T(1,128)S(1)}, f32[4,1,256]{2,1,0:T(1,128)S(1)}, u32[]{:S(2)}, u32[]{:S(2)}) collective-permute-start(f32[4,1,256]{2,1,0:T(1,128)S(1)} %get-tuple-element.68), channel_id=1, source_target_pairs={{1,0},{3,2},{5,4},{7,6},{9,8},{11,10},{13,12},{15,14},{17,16},{19,... | collective-permute-start | bytes 12296 | tf_op jit(solution)/shard_map/ppermute | solution.py:27
  63.5 3.2 %collective-permute-start.9 = (f32[4,1,256]{2,1,0:T(1,128)S(1)}, f32[4,1,256]{2,1,0:T(1,128)S(1)}, u32[]{:S(2)}, u32[]{:S(2)}) collective-permute-start(f32[4,1,256]{2,1,0:T(1,128)S(1)} %get-tuple-element.67), channel_id=1, source_target_pairs={{0,1},{2,3},{4,5},{6,7},{8,9},{10,11},{12,13},{14,15},{16,17},{18,... | collective-permute-start | bytes 12296 | tf_op jit(solution)/shard_map/ppermute | solution.py:26
  65.2 5.5 %collective-permute-start.8 = (f32[4,1,256]{2,1,0:T(1,128)S(1)}, f32[4,1,256]{2,1,0:T(1,128)S(1)}, u32[]{:S(2)}, u32[]{:S(2)}) collective-permute-start(f32[4,1,256]{2,1,0:T(1,128)S(1)} %get-tuple-element.66), channel_id=1, source_target_pairs={{1,0},{3,2},{5,4},{7,6},{9,8},{11,10},{13,12},{15,14},{17,16},{19,... | collective-permute-start | bytes 12296 | tf_op jit(solution)/shard_map/ppermute | solution.py:27
  71.6 3.2 %collective-permute-start.11 = (f32[4,1,256]{2,1,0:T(1,128)S(1)}, f32[4,1,256]{2,1,0:T(1,128)S(1)}, u32[]{:S(2)}, u32[]{:S(2)}) collective-permute-start(f32[4,1,256]{2,1,0:T(1,128)S(1)} %get-tuple-element.65), channel_id=1, source_target_pairs={{0,1},{2,3},{4,5},{6,7},{8,9},{10,11},{12,13},{14,15},{16,17},{18,... | collective-permute-start | bytes 12296 | tf_op jit(solution)/shard_map/ppermute | solution.py:26
  73.2 5.5 %collective-permute-start.10 = (f32[4,1,256]{2,1,0:T(1,128)S(1)}, f32[4,1,256]{2,1,0:T(1,128)S(1)}, u32[]{:S(2)}, u32[]{:S(2)}) collective-permute-start(f32[4,1,256]{2,1,0:T(1,128)S(1)} %get-tuple-element.64), channel_id=1, source_target_pairs={{1,0},{3,2},{5,4},{7,6},{9,8},{11,10},{13,12},{15,14},{17,16},{19,... | collective-permute-start | bytes 12296 | tf_op jit(solution)/shard_map/ppermute | solution.py:27
  79.6 3.2 %collective-permute-start.13 = (f32[4,1,256]{2,1,0:T(1,128)S(1)}, f32[4,1,256]{2,1,0:T(1,128)S(1)}, u32[]{:S(2)}, u32[]{:S(2)}) collective-permute-start(f32[4,1,256]{2,1,0:T(1,128)S(1)} %get-tuple-element.63), channel_id=1, source_target_pairs={{0,1},{2,3},{4,5},{6,7},{8,9},{10,11},{12,13},{14,15},{16,17},{18,... | collective-permute-start | bytes 12296 | tf_op jit(solution)/shard_map/ppermute | solution.py:26
  81.3 5.5 %collective-permute-start.12 = (f32[4,1,256]{2,1,0:T(1,128)S(1)}, f32[4,1,256]{2,1,0:T(1,128)S(1)}, u32[]{:S(2)}, u32[]{:S(2)}) collective-permute-start(f32[4,1,256]{2,1,0:T(1,128)S(1)} %get-tuple-element.62), channel_id=1, source_target_pairs={{1,0},{3,2},{5,4},{7,6},{9,8},{11,10},{13,12},{15,14},{17,16},{19,... | collective-permute-start | bytes 12296 | tf_op jit(solution)/shard_map/ppermute | solution.py:27
  87.7 3.2 %collective-permute-start.15 = (f32[4,1,256]{2,1,0:T(1,128)S(1)}, f32[4,1,256]{2,1,0:T(1,128)S(1)}, u32[]{:S(2)}, u32[]{:S(2)}) collective-permute-start(f32[4,1,256]{2,1,0:T(1,128)S(1)} %get-tuple-element.61), channel_id=1, source_target_pairs={{0,1},{2,3},{4,5},{6,7},{8,9},{10,11},{12,13},{14,15},{16,17},{18,... | collective-permute-start | bytes 12296 | tf_op jit(solution)/shard_map/ppermute | solution.py:26
  89.4 5.5 %collective-permute-start.14 = (f32[4,1,256]{2,1,0:T(1,128)S(1)}, f32[4,1,256]{2,1,0:T(1,128)S(1)}, u32[]{:S(2)}, u32[]{:S(2)}) collective-permute-start(f32[4,1,256]{2,1,0:T(1,128)S(1)} %get-tuple-element.60), channel_id=1, source_target_pairs={{1,0},{3,2},{5,4},{7,6},{9,8},{11,10},{13,12},{15,14},{17,16},{19,... | collective-permute-start | bytes 12296 | tf_op jit(solution)/shard_map/ppermute | solution.py:27
  95.8 3.2 %collective-permute-start.17 = (f32[4,1,256]{2,1,0:T(1,128)S(1)}, f32[4,1,256]{2,1,0:T(1,128)S(1)}, u32[]{:S(2)}, u32[]{:S(2)}) collective-permute-start(f32[4,1,256]{2,1,0:T(1,128)S(1)} %get-tuple-element.59), channel_id=1, source_target_pairs={{0,1},{2,3},{4,5},{6,7},{8,9},{10,11},{12,13},{14,15},{16,17},{18,... | collective-permute-start | bytes 12296 | tf_op jit(solution)/shard_map/ppermute | solution.py:26
  97.4 5.5 %collective-permute-start.16 = (f32[4,1,256]{2,1,0:T(1,128)S(1)}, f32[4,1,256]{2,1,0:T(1,128)S(1)}, u32[]{:S(2)}, u32[]{:S(2)}) collective-permute-start(f32[4,1,256]{2,1,0:T(1,128)S(1)} %get-tuple-element.58), channel_id=1, source_target_pairs={{1,0},{3,2},{5,4},{7,6},{9,8},{11,10},{13,12},{15,14},{17,16},{19,... | collective-permute-start | bytes 12296 | tf_op jit(solution)/shard_map/ppermute | solution.py:27
  103.8 3.2 %collective-permute-start.19 = (f32[4,1,256]{2,1,0:T(1,128)S(1)}, f32[4,1,256]{2,1,0:T(1,128)S(1)}, u32[]{:S(2)}, u32[]{:S(2)}) collective-permute-start(f32[4,1,256]{2,1,0:T(1,128)S(1)} %get-tuple-element.57), channel_id=1, source_target_pairs={{0,1},{2,3},{4,5},{6,7},{8,9},{10,11},{12,13},{14,15},{16,17},{18,... | collective-permute-start | bytes 12296 | tf_op jit(solution)/shard_map/ppermute | solution.py:26
  105.5 5.5 %collective-permute-start.18 = (f32[4,1,256]{2,1,0:T(1,128)S(1)}, f32[4,1,256]{2,1,0:T(1,128)S(1)}, u32[]{:S(2)}, u32[]{:S(2)}) collective-permute-start(f32[4,1,256]{2,1,0:T(1,128)S(1)} %get-tuple-element.56), channel_id=1, source_target_pairs={{1,0},{3,2},{5,4},{7,6},{9,8},{11,10},{13,12},{15,14},{17,16},{19,... | collective-permute-start | bytes 12296 | tf_op jit(solution)/shard_map/ppermute | solution.py:27
  111.5 1.8 %collective-permute-start.20 = (f32[2,3,64,256]{3,2,1,0:T(8,128)S(1)}, f32[2,3,64,256]{3,2,1,0:T(8,128)S(1)}, u32[]{:S(2)}, u32[]{:S(2)}) collective-permute-start(f32[2,3,64,256]{3,2,1,0:T(8,128)S(1)} %pad_maximum_fusion.3), channel_id=1, source_target_pairs={{0,2},{2,0},{4,6},{6,4},{8,10},{10,8},{12,14},{14,12},{16,18},{18,... | collective-permute-start | bytes 1179656 | tf_op jit(solution)/shard_map/ppermute | solution.py:16
  113.4 11.2 %collective-permute-start.21 = (f32[2,3,64,256]{3,2,1,0:T(8,128)S(1)}, f32[2,3,64,256]{3,2,1,0:T(8,128)S(1)}, u32[]{:S(2)}, u32[]{:S(2)}) collective-permute-start(f32[2,3,64,256]{3,2,1,0:T(8,128)S(1)} %pad_maximum_fusion.4), channel_id=1, source_target_pairs={{0,4},{2,6},{4,0},{6,2},{8,12},{10,14},{12,8},{14,10},{16,20},{18,... | collective-permute-start | bytes 1179656 | tf_op jit(solution)/shard_map/ppermute | solution.py:16
  124.8 11.1 %collective-permute-start.22 = (f32[2,3,64,256]{3,2,1,0:T(8,128)S(1)}, f32[2,3,64,256]{3,2,1,0:T(8,128)S(1)}, u32[]{:S(2)}, u32[]{:S(2)}) collective-permute-start(f32[2,3,64,256]{3,2,1,0:T(8,128)S(1)} %pad_maximum_fusion.5), channel_id=1, source_target_pairs={{0,8},{2,10},{4,12},{6,14},{8,0},{10,2},{12,4},{14,6},{16,24},{18,... | collective-permute-start | bytes 1179656 | tf_op jit(solution)/shard_map/ppermute | solution.py:16
  136.1 19.9 %collective-permute-start.23 = (f32[2,3,64,256]{3,2,1,0:T(8,128)S(1)}, f32[2,3,64,256]{3,2,1,0:T(8,128)S(1)}, u32[]{:S(2)}, u32[]{:S(2)}) collective-permute-start(f32[2,3,64,256]{3,2,1,0:T(8,128)S(1)} %pad_maximum_fusion.6), channel_id=1, source_target_pairs={{0,16},{2,18},{4,20},{6,22},{8,24},{10,26},{12,28},{14,30},{16,0},... | collective-permute-start | bytes 1179656 | tf_op jit(solution)/shard_map/ppermute | solution.py:16
  (3 other events, 25.7 us)
where the time goes:
time: 157 us
  waiting for transfers between devices  102 us (65%)
  starting transfers between devices  39.8 us (25%)
  other arithmetic  6.61 us (4%)
  local copies, waits for them, and re-layouts  6.01 us (4%)
  between operations  2.04 us (1%)
    ppermute x8, waiting for transfers between devices, partner_2(): lax.ppermute(x, axis, [(i, i ^ 1 << stride) for i in range(lax.axis_size(...  71.6 us
    ppermute x8, waiting for transfers between devices, extended(): after = lax.ppermute(initial, axis, down)  30.5 us
    ppermute x8, starting transfers between devices, extended(): before = lax.ppermute(last, axis, up)  15.3 us
    ppermute x8, starting transfers between devices, partner_2(): lax.ppermute(x, axis, [(i, i ^ 1 << stride) for i in range(lax.axis_size(...  14.2 us
    ppermute x8, starting transfers between devices, extended(): after = lax.ppermute(initial, axis, down)  10.3 us
  transfers between devices with their start and end apart: 24, of which 16 were waited for; matrix products, arithmetic and copies ran while one was open for 2% of the time, Pallas kernels for 0%

commit v1 on v0

v1 whole, which is shorter than its diff:
```python
import functools

import jax
import jax.numpy as jnp
import numpy as np
from jax import lax
from jax.experimental import pallas as pl
from jax.experimental.pallas import tpu as pltpu
from jax.sharding import PartitionSpec as P

SWEEPS = 8
RHO = 0.9
SIGMA = 0.01
TERMS = SWEEPS + 1
HALO = 8
MESH = pl.DeviceIdType.MESH


def coefficients(window):
    k = np.arange(window)
    lam = 1.0 - RHO * np.exp(-2j * np.pi * k / window)
    gap = np.arange(-(window - 1), window)
    phase = np.exp(2j * np.pi * gap[:, None] * k[None, :] / window)
    powers = np.stack([lam ** -(n + 1.0) for n in range(TERMS)])
    table = (powers @ phase.T).real / window * RHO ** (-gap.astype(np.float64))
    return table.astype(np.float32)


def gather_kernel(window, rows, coef, rhs, depth, coriolis, out, main, halo, plane, z_acc, send_main, recv_main,
                  send_halo, recv_halo, send_y, recv_y):
    tm, y = lax.axis_index("tm"), lax.axis_index("space")
    z, x, c = tm // 4, tm % 4 // 2, tm % 2
    end = (z == 0) | (z == 3)
    pair = z + 1 - 2 * (z % 2)
    third = jnp.where(z < 2, 2, 1)
    fourth = jnp.where(z < 2, 3, 0)
    order = [z, pair, third, fourth]
    x_other, c_other = z * 4 + (1 - x) * 2 + c, z * 4 + x * 2 + 1 - c

    barrier = pltpu.get_barrier_semaphore()
    for peer in (x_other, c_other):
        pl.semaphore_signal(barrier, inc=1, device_id={"tm": peer}, device_id_type=MESH)
    pl.semaphore_signal(barrier, inc=1, device_id={"space": 1 - y}, device_id_type=MESH)

    @pl.when(z > 0)
    def _():
        pl.semaphore_signal(barrier, inc=1, device_id={"tm": tm - 4}, device_id_type=MESH)

    @pl.when(z < 3)
    def _():
        pl.semaphore_signal(barrier, inc=1, device_id={"tm": tm + 4}, device_id_type=MESH)

    main[tm] = rhs[0]
    plane[0, :rows] = -SIGMA * depth[...]
    plane[1, :rows] = coriolis[...]
    pl.semaphore_wait(barrier, jnp.where(end, 4, 5))

    kinds = ((main, send_main, recv_main), (halo, send_halo, recv_halo))
    pending = []

    def copy(kind, block, slot, peer):
        buf, send, recv = kinds[kind]
        return pltpu.make_async_remote_copy(
            src_ref=buf.at[block], dst_ref=buf.at[block], send_sem=send.at[slot], recv_sem=recv.at[block],
            device_id={"tm": peer}, device_id_type=MESH)

    slots = [0, 0]

    def send(kind, block, peer, when=None):
        slot = slots[kind]
        slots[kind] += 1
        def start():
            copy(kind, block, slot, peer).start()
        def finish():
            copy(kind, block, slot, peer).wait_send()
        if when is None:
            start()
            pending.append(finish)
        else:
            pl.when(when)(start)
            pending.append(lambda: pl.when(when)(finish))

    def arrived(kind, block):
        copy(kind, block, 0, c_other).wait_recv()

    def block_of(zz, same_x, same_c):
        return zz * 4 + (x if same_x else 1 - x) * 2 + (c if same_c else 1 - c)

    edge = pl.multiple_of((1 - y) * (rows - HALO), HALO)
    edges = pltpu.make_async_remote_copy(
        src_ref=main.at[tm, :, pl.ds(edge, HALO), :], dst_ref=halo.at[tm], send_sem=send_y.at[0],
        recv_sem=recv_halo.at[tm], device_id={"space": 1 - y}, device_id_type=MESH)
    fixed = pltpu.make_async_remote_copy(
        src_ref=plane.at[:, pl.ds(edge, HALO), :], dst_ref=plane.at[:, pl.ds(rows, HALO), :], send_sem=send_y.at[1],
        recv_sem=recv_y.at[0], device_id={"space": 1 - y}, device_id_type=MESH)
    edges.start()

    def send_own(kind):
        send(kind, tm, tm + 4, z < 3)
        send(kind, tm, tm - 4, z > 0)
        send(kind, tm, x_other)
        send(kind, tm, c_other)

    def relay_z(kind, stage):
        zz = order[stage]
        block = block_of(zz, True, True)
        arrived(kind, block)
        onward = jnp.where(zz < z, z + 1, z - 1)
        if stage > 0:
            send(kind, block, onward * 4 + x * 2 + c, (onward >= 0) & (onward <= 3))
        send(kind, block, x_other, (end & (c == 1)) if stage == 1 else None)
        send(kind, block, c_other)

    def relay_x(kind, stage):
        block = block_of(order[stage], False, True)
        arrived(kind, block)
        if stage == 0:
            send(kind, block, pair * 4 + x * 2 + c, end | (c == 0))
        send(kind, block, c_other)

    def accumulate(stage):
        blocks = [order[stage] * 4 + q for q in range(4)]
        weights = [[coef[n, tm - b + window - 1] for b in blocks] for n in range(TERMS)]
        step = 32

        def add(parts, n, field, lo, size):
            total = parts[0] * weights[n][0]
            for q in range(1, 4):
                total = total + parts[q] * weights[n][q]
            if stage > 0:
                total = total + z_acc[n, field, lo:lo + size]
            z_acc[n, field, lo:lo + size] = total

        def body(field, carry):
            for lo in range(0, rows, step):
                parts = [main[b, field, lo:lo + step] for b in blocks]
                for n in range(TERMS):
                    add(parts, n, field, lo, step)
            parts = [halo[b, field] for b in blocks]
            for n in range(TERMS):
                add(parts, n, field, rows, HALO)
            return carry

        lax.fori_loop(0, 3, body, 0)

    send_own(0)
    fixed.start()
    edges.wait_recv()
    send_own(1)
    for stage in range(4):
        if stage < 3:
            for kind in (0, 1):
                relay_z(kind, stage + 1)
        for kind in (0, 1):
            relay_x(kind, stage)
        for kind in (0, 1):
            arrived(kind, block_of(order[stage], True, False))
            arrived(kind, block_of(order[stage], False, False))
        accumulate(stage)
    fixed.wait_recv()

    full = rows + HALO
    line = lax.broadcasted_iota(jnp.int32, (full, 256), 0)
    above = jnp.where((line == 0) & (y == 0), 0.0, 1.0)
    below = jnp.where((line == rows - 1) & (y == 1), 0.0, 1.0)

    def dx(a):
        return pltpu.roll(a, full - 1, 0) * below - pltpu.roll(a, 1, 0) * above

    def dy(a):
        return pltpu.roll(a, a.shape[1] - 1, 1) - pltpu.roll(a, 1, 1)

    h, u, v = z_acc[SWEEPS, 0], z_acc[SWEEPS, 1], z_acc[SWEEPS, 2]
    for n in reversed(range(SWEEPS)):
        scaled_depth, turn = plane[0], plane[1]
        h, u, v = (
            z_acc[n, 0] + scaled_depth * (dx(u) + dy(v)),
            z_acc[n, 1] - SIGMA * dx(h) + turn * v,
            z_acc[n, 2] - SIGMA * dy(h) - turn * u,
        )
    out[0, 0] = h[:rows]
    out[0, 1] = u[:rows]
    out[0, 2] = v[:rows]

    for finish in pending:
        finish()
    edges.wait_send()
    fixed.wait_send()


def shards_kernel(rhs, depth, coriolis):
    window = lax.axis_size("tm")
    _, fields, rows, columns = rhs.shape
    vmem = pl.BlockSpec(memory_space=pltpu.VMEM)
    dma = pltpu.SemaphoreType.DMA
    return pl.pallas_call(
        functools.partial(gather_kernel, window, rows),
        out_shape=jax.ShapeDtypeStruct(rhs.shape, jnp.float32),
        in_specs=[pl.BlockSpec(memory_space=pltpu.SMEM), vmem, vmem, vmem],
        out_specs=vmem,
        scratch_shapes=[
            pltpu.VMEM((window, fields, rows, columns), jnp.float32),
            pltpu.VMEM((window, fields, HALO, columns), jnp.float32),
            pltpu.VMEM((2, rows + HALO, columns), jnp.float32),
            pltpu.VMEM((TERMS, fields, rows + HALO, columns), jnp.float32),
            dma((24,)), dma((window,)), dma((24,)), dma((window,)), dma((2,)), dma((1,)),
        ],
        compiler_params=pltpu.CompilerParams(collective_id=0, has_side_effects=True, vmem_limit_bytes=48 << 20),
        cost_estimate=pl.CostEstimate(flops=40_000_000, bytes_accessed=1_000_000, transcendentals=0),
    )(jnp.asarray(coefficients(window)), rhs, depth, coriolis)


def shards_plain(rhs, depth, coriolis):
    window, tiles = lax.axis_size("tm"), lax.axis_size("space")
    tm = lax.axis_index("tm")

    def widen(a, dim):
        length = a.shape[dim]
        last = lax.slice_in_dim(a, length - HALO, length, axis=dim)
        first = lax.slice_in_dim(a, 0, HALO, axis=dim)
        before = lax.ppermute(last, "space", [(i, i + 1) for i in range(tiles - 1)])
        after = lax.ppermute(first, "space", [(i + 1, i) for i in range(tiles - 1)])
        return jnp.concatenate([before, a, after], axis=dim)

    table = jnp.asarray(coefficients(window))
    mine = lax.dynamic_slice_in_dim(table, tm, window, axis=1)[:, ::-1]
    wide = widen(rhs[0], 1)
    everyone = lax.all_gather(wide, "tm")
    sums = jnp.einsum("nj,jfxy->nfxy", mine, everyone, precision=lax.Precision.HIGHEST)
    rows = rhs.shape[2]
    line = lax.axis_index("space") * rows - HALO + jnp.arange(rows + 2 * HALO)
    inside = ((line >= 0) & (line < rows * tiles)).astype(jnp.float32)[:, None]
    deep, turn = -SIGMA * widen(depth, 0), widen(coriolis, 0)

    def dx(a):
        return (jnp.roll(a, -1, 0) - jnp.roll(a, 1, 0)) * inside

    def dy(a):
        return jnp.roll(a, -1, 1) - jnp.roll(a, 1, 1)

    h, u, v = sums[SWEEPS]
    for n in reversed(range(SWEEPS)):
        h, u, v = (sums[n, 0] + deep * (dx(u) + dy(v)), sums[n, 1] - SIGMA * dx(h) + turn * v,
                   sums[n, 2] - SIGMA * dy(h) - turn * u)
    return jnp.stack([h, u, v])[None, :, HALO:rows + HALO]


def solution(mesh):
    in_specs = (P("tm", None, "space", None), P("space", None), P("space", None))
    out_specs = P("tm", None, "space", None)
    body = shards_kernel if (mesh.shape["tm"], mesh.shape["space"]) == (16, 2) else shards_plain
    return jax.shard_map(body, mesh=mesh, in_specs=in_specs, out_specs=out_specs, check_vma=False)
```

time: 157 us -> 38.6 us (0.25)
  waiting for transfers between devices: 102 us -> 0 us
  starting transfers between devices: 39.8 us -> 0 us
  Pallas kernels: 0 us -> 34.2 us
  other arithmetic: 6.61 us -> 0 us
  between operations: 2.04 us -> 0.01 us
  local copies, waits for them, and re-layouts: 6.01 us -> 3.98 us
    ppermute x24 -> x0, waiting for transfers between devices: 102 us -> none  [the longest x8 71.6 us: partner_2(): lax.ppermute(x, axis, [(i, i ^ 1 << stride) for i in range(lax.axis_size(...]
    ppermute x24 -> x0, starting transfers between devices: 39.8 us -> none  [the longest x8 15.3 us: extended(): before = lax.ppermute(last, axis, up)]
    pallas_call x0 -> x1, Pallas kernels: none -> 34.2 us  [shards_kernel(): pl.pallas_call(functools.partial(gather_kernel, window, rows), out_shape=...]
    slice x78 -> x0, local copies, waits for them, and re-layouts: 5 us -> none  [the longest x32 2.46 us: tendency(): north_dy = jnp.roll(north, -1, axis=1) - jnp.roll(north, 1, axis=1)]
    unnamed x6 -> x9, local copies, waits for them, and re-layouts: 0.77 us -> 3.98 us
    another operation x39 -> x0, other arithmetic: 3.14 us -> none  [the longest x32 2.94 us: tendency(): jnp.stack([-SIGMA * depth * (east_dx + north_dy), -SIGMA * height_dx + co...]
    mul x2 -> x0, other arithmetic: 1.69 us -> none  [the longest x1 0.94 us: shards(): scaled = rhs[0] * jnp.power(jnp.float32(RHO), moment)]
  transfers between devices with their start and end apart: 24 -> 0, of which waited for: 16 -> 0; matrix products, arithmetic and copies ran while one was open for 2% -> 0% of each run, Pallas kernels for 0% -> 0%
where the time goes in v1:
time: 38.6 us; the launch traced here: 38.2 us
  Pallas kernels  34.2 us (89%)
  local copies, waits for them, and re-layouts  3.98 us (10%)
    pallas_call x1, Pallas kernels, shards_kernel(): pl.pallas_call(functools.partial(gather_kernel, window, rows), out_shape=...  34.2 us
    unnamed x9, local copies, waits for them, and re-layouts  3.98 us

profile of v1, /device:TPU:0, one launch (start us, length us, event | category | flops | bytes accessed | tf_op | source)
XLA Modules:
  0.0 38.2 jit_solution(1783918920719133505)
XLA Ops:
  0.0 0.0 copy-start
  0.0 0.9 %copy-done = f32[1,3,64,256]{3,2,1,0:T(8,128)S(1)} copy-done((f32[1,3,64,256]{3,2,1,0:T(8,128)S(1)}, f32[1,3,64,256]{3,2,1,0:T(8,128)}, u32[]{:S(2)}) %copy-start) | copy-done | bytes 196632
  0.9 0.0 copy-start.1
  0.9 0.8 %copy-done.1 = f32[64,256]{1,0:T(8,128)S(1)} copy-done((f32[64,256]{1,0:T(8,128)S(1)}, f32[64,256]{1,0:T(8,128)}, u32[]{:S(2)}) %copy-start.1) | copy-done | bytes 65560
  1.8 0.0 copy-start.2
  1.8 0.8 %copy-done.2 = f32[64,256]{1,0:T(8,128)S(1)} copy-done((f32[64,256]{1,0:T(8,128)S(1)}, f32[64,256]{1,0:T(8,128)}, u32[]{:S(2)}) %copy-start.2) | copy-done | bytes 65560
  2.6 0.0 copy-start.3
  2.6 0.7 %copy-done.3 = f32[9,31]{1,0:T(8,128)S(1)} copy-done((f32[9,31]{1,0:T(8,128)S(1)}, f32[9,31]{1,0:T(8,128)}, u32[]{:S(2)}) %copy-start.3) | copy-done | bytes 1140
  3.3 34.2 %shard_map.46 = f32[1,3,64,256]{3,2,1,0:T(8,128)S(1)} custom-call(f32[9,31]{1,0:T(8,128)S(1)} %copy-done.3, f32[1,3,64,256]{3,2,1,0:T(8,128)S(1)} %copy-done, f32[64,256]{1,0:T(8,128)S(1)} %copy-done.1, f32[64,256]{1,0:T(8,128)S(1)} %copy-done.2), custom_call_target="tpu_custom_call" | custom-call | flops 40000000 | bytes 1000000 | tf_op jit(solution)/shard_map/pallas_call | solution.py:196
  37.5 0.7 %copy.6 = f32[1,3,64,256]{3,2,1,0:T(8,128)} copy(f32[1,3,64,256]{3,2,1,0:T(8,128)S(1)} %shard_map.46) | data formatting | bytes 393216
Async XLA Ops:
  0.0 0.9 %copy-start = (f32[1,3,64,256]{3,2,1,0:T(8,128)S(1)}, f32[1,3,64,256]{3,2,1,0:T(8,128)}, u32[]{:S(2)}) copy-start(f32[1,3,64,256]{3,2,1,0:T(8,128)} %rhs.1) | copy-start | bytes 589828
  0.9 0.8 %copy-start.1 = (f32[64,256]{1,0:T(8,128)S(1)}, f32[64,256]{1,0:T(8,128)}, u32[]{:S(2)}) copy-start(f32[64,256]{1,0:T(8,128)} %depth.1) | copy-start | bytes 196612
  1.8 0.8 %copy-start.2 = (f32[64,256]{1,0:T(8,128)S(1)}, f32[64,256]{1,0:T(8,128)}, u32[]{:S(2)}) copy-start(f32[64,256]{1,0:T(8,128)} %coriolis.1) | copy-start | bytes 196612
  2.6 0.7 %copy-start.3 = (f32[9,31]{1,0:T(8,128)S(1)}, f32[9,31]{1,0:T(8,128)}, u32[]{:S(2)}) copy-start(f32[9,31]{1,0:T(8,128)} %constant.2.clone.coef) | copy-start | bytes 3352

commit v2 on v1

v2 whole, which is shorter than its diff:
```python
import functools

import jax
import jax.numpy as jnp
import numpy as np
from jax import lax
from jax.experimental import pallas as pl
from jax.experimental.pallas import tpu as pltpu
from jax.sharding import PartitionSpec as P

SWEEPS = 8
RHO = 0.9
SIGMA = 0.01
TERMS = SWEEPS + 1
HALO = 8
MESH = pl.DeviceIdType.MESH


def coefficients(window):
    k = np.arange(window)
    lam = 1.0 - RHO * np.exp(-2j * np.pi * k / window)
    gap = np.arange(-(window - 1), window)
    phase = np.exp(2j * np.pi * gap[:, None] * k[None, :] / window)
    powers = np.stack([lam ** -(n + 1.0) for n in range(TERMS)])
    table = (powers @ phase.T).real / window * RHO ** (-gap.astype(np.float64))
    return table.astype(np.float32)


def gather_kernel(window, rows, table, rhs, depth, coriolis, out, main, plane, z_acc, coef, send_sem, send_own, recv_sem,
                  local_sem, send_y, recv_y):
    tm, y = lax.axis_index("tm"), lax.axis_index("space")
    z, x, c = tm // 4, tm % 4 // 2, tm % 2
    end = (z == 0) | (z == 3)
    inner = jnp.logical_not(end)
    fields = range(3)
    pair = z + 1 - 2 * (z % 2)
    order = [z, pair, jnp.where(z < 2, 2, 1), jnp.where(z < 2, 3, 0)]
    x_other, c_other = z * 4 + (1 - x) * 2 + c, z * 4 + x * 2 + 1 - c

    loads = [
        pltpu.make_async_copy(rhs.at[0], main.at[tm, :, pl.ds(0, rows), :], local_sem.at[0]),
        pltpu.make_async_copy(depth, plane.at[0, pl.ds(0, rows), :], local_sem.at[1]),
        pltpu.make_async_copy(coriolis, plane.at[1, pl.ds(0, rows), :], local_sem.at[2]),
    ]
    for load in loads:
        load.start()

    barrier = pltpu.get_barrier_semaphore()
    for peer in (x_other, c_other):
        pl.semaphore_signal(barrier, inc=1, device_id={"tm": peer}, device_id_type=MESH)
    pl.semaphore_signal(barrier, inc=1, device_id={"space": 1 - y}, device_id_type=MESH)

    @pl.when(z > 0)
    def _():
        pl.semaphore_signal(barrier, inc=1, device_id={"tm": tm - 4}, device_id_type=MESH)

    @pl.when(z < 3)
    def _():
        pl.semaphore_signal(barrier, inc=1, device_id={"tm": tm + 4}, device_id_type=MESH)

    for n in range(TERMS):
        for gap in range(2 * window - 1):
            coef[n, gap] = float(table[n, gap])
    for load in loads:
        load.wait()
    pl.semaphore_wait(barrier, jnp.where(end, 4, 5))

    pending = []
    both = lambda *conds: functools.reduce(jnp.logical_and, conds) if conds else None

    def guarded(when, act):
        if when is None:
            act()
        else:
            pl.when(when)(act)

    def copy(block, f, slot, peer):
        return pltpu.make_async_remote_copy(
            src_ref=main.at[block, f], dst_ref=main.at[block, f], send_sem=send_sem.at[slot],
            recv_sem=recv_sem.at[block, f], device_id={"tm": peer}, device_id_type=MESH)

    slots = {}

    def send(key, block, f, peer, start_when=None, finish_when=None):
        fresh = key not in slots
        slot = slots.setdefault(key, len(slots))
        guarded(start_when, lambda: copy(block, f, slot, peer).start())
        if fresh:
            pending.append(lambda: guarded(finish_when, lambda: copy(block, f, slot, peer).wait_send()))

    def arrived(block, f):
        copy(block, f, 0, c_other).wait_recv()

    def block_of(stage, same_x, same_c):
        return order[stage] * 4 + (x if same_x else 1 - x) * 2 + (c if same_c else 1 - c)

    edge = pl.multiple_of((1 - y) * (rows - HALO), HALO)
    tail = pl.ds(rows, HALO)
    edges = pltpu.make_async_remote_copy(
        src_ref=main.at[tm, :, pl.ds(edge, HALO), :], dst_ref=main.at[tm, :, tail, :], send_sem=send_y.at[0],
        recv_sem=recv_y.at[0], device_id={"space": 1 - y}, device_id_type=MESH)
    fixed = pltpu.make_async_remote_copy(
        src_ref=plane.at[:, pl.ds(edge, HALO), :], dst_ref=plane.at[:, tail, :], send_sem=send_y.at[1],
        recv_sem=recv_y.at[1], device_id={"space": 1 - y}, device_id_type=MESH)
    edges.start()

    def own(f, part, index):
        for q, (peer, when) in enumerate([(tm + 4, z < 3), (tm - 4, z > 0), (x_other, None), (c_other, None)]):
            def make(peer=peer, q=q):
                ref = main.at[tm, f, part, :]
                return pltpu.make_async_remote_copy(
                    src_ref=ref, dst_ref=ref, send_sem=send_own.at[index, q], recv_sem=recv_sem.at[tm, f],
                    device_id={"tm": peer}, device_id_type=MESH)
            guarded(when, lambda make=make: make().start())
            pending.append(lambda when=when, make=make: guarded(when, lambda: make().wait_send()))

    def relay_z(stage, f, when=None):
        block = block_of(stage, True, True)
        guarded(when, lambda: arrived(block, f))
        conds = [] if when is None else [when]
        onward = jnp.where(order[stage] < z, z + 1, z - 1)
        send(("z", stage, f), block, f, onward * 4 + x * 2 + c, both(inner, *conds), inner)
        cross = [end & (c == 1)] if stage == 1 else []
        send(("x", stage, f), block, f, x_other, both(*cross, *conds), both(*cross))
        send(("c", stage, f), block, f, c_other, both(*conds))

    def relay_x(stage, f, when=None):
        block = block_of(stage, False, True)
        guarded(when, lambda: arrived(block, f))
        send(("cx", stage, f), block, f, c_other, when)

    def second_route(f, when):
        send(("zx", f), block_of(0, False, True), f, pair * 4 + x * 2 + c, when, end | (c == 0))

    def accumulate(stage, f, first=False):
        arrived(block_of(stage, True, False), f)
        arrived(block_of(stage, False, False), f)
        blocks = [order[stage] * 4 + q for q in range(4)]
        weights = [[coef[n, tm - b + window - 1] for b in blocks] for n in range(TERMS)]
        step = 24

        def body(i, carry):
            part = pl.ds(pl.multiple_of(i * step, 8), step)
            parts = [main[b, f, part] for b in blocks]
            for n in range(TERMS):
                total = parts[0] * weights[n][0]
                for q in range(1, 4):
                    total = total + parts[q] * weights[n][q]
                if not first:
                    total = total + z_acc[n, f, part]
                z_acc[n, f, part] = total
            return carry

        lax.fori_loop(0, (rows + HALO) // step, body, 0)

    body_rows = pl.ds(0, rows)
    own(0, body_rows, 0)
    own(1, body_rows, 1)
    edges.wait_recv()
    own(0, tail, 3)
    own(1, tail, 4)
    own(2, body_rows, 2)
    own(2, tail, 5)
    fixed.start()

    late = end & (c == 0)
    for f in fields:
        relay_z(1, f)
        relay_z(2, f, inner)
        relay_x(0, f)
        second_route(f, end)
    for f in fields:
        relay_z(2, f, end)
        relay_z(3, f, inner)
        relay_x(1, f, jnp.logical_not(late))
        relay_x(2, f, inner)
        accumulate(0, f, first=True)
    for f in fields:
        second_route(f, inner & (c == 0))
    for f in fields:
        relay_z(3, f, end)
        relay_x(2, f, end)
        relay_x(3, f, inner)
    for f in fields:
        relay_x(3, f, end)
        accumulate(2, f)
    for f in fields:
        relay_x(1, f, late)
        accumulate(3, f)
    for f in fields:
        accumulate(1, f)
    fixed.wait_recv()
    fixed.wait_send()

    full = rows + HALO
    line = lax.broadcasted_iota(jnp.int32, (full, 256), 0)
    above = jnp.where((line == 0) & (y == 0), 0.0, 1.0)
    below = jnp.where((line == rows - 1) & (y == 1), 0.0, 1.0)

    def dx(a):
        return pltpu.roll(a, full - 1, 0) * below - pltpu.roll(a, 1, 0) * above

    def dy(a):
        return pltpu.roll(a, a.shape[1] - 1, 1) - pltpu.roll(a, 1, 1)

    plane[0] = -SIGMA * plane[0]
    h, u, v = z_acc[SWEEPS, 0], z_acc[SWEEPS, 1], z_acc[SWEEPS, 2]
    for n in reversed(range(SWEEPS)):
        scaled_depth, turn = plane[0], plane[1]
        h, u, v = (
            z_acc[n, 0] + scaled_depth * (dx(u) + dy(v)),
            z_acc[n, 1] - SIGMA * dx(h) + turn * v,
            z_acc[n, 2] - SIGMA * dy(h) - turn * u,
        )
    out[0, 0] = h[:rows]
    out[0, 1] = u[:rows]
    out[0, 2] = v[:rows]

    for finish in pending:
        finish()
    edges.wait_send()


def shards_kernel(rhs, depth, coriolis):
    window = lax.axis_size("tm")
    _, fields, rows, columns = rhs.shape
    far = pl.BlockSpec(memory_space=pltpu.HBM)
    dma = pltpu.SemaphoreType.DMA
    return pl.pallas_call(
        functools.partial(gather_kernel, window, rows, coefficients(window)),
        out_shape=jax.ShapeDtypeStruct(rhs.shape, jnp.float32),
        in_specs=[far, far, far],
        out_specs=pl.BlockSpec(memory_space=pltpu.VMEM),
        scratch_shapes=[
            pltpu.VMEM((window, fields, rows + HALO, columns), jnp.float32),
            pltpu.VMEM((2, rows + HALO, columns), jnp.float32),
            pltpu.VMEM((TERMS, fields, rows + HALO, columns), jnp.float32),
            pltpu.SMEM((TERMS, 2 * window - 1), jnp.float32),
            dma((48,)), dma((6, 4)), dma((window, fields)), dma((3,)), dma((2,)), dma((2,)),
        ],
        compiler_params=pltpu.CompilerParams(collective_id=0, has_side_effects=True, vmem_limit_bytes=62 << 20),
        cost_estimate=pl.CostEstimate(flops=40_000_000, bytes_accessed=1_000_000, transcendentals=0),
    )(rhs, depth, coriolis)


def shards_plain(rhs, depth, coriolis):
    window, tiles = lax.axis_size("tm"), lax.axis_size("space")
    tm = lax.axis_index("tm")

    def widen(a, dim):
        length = a.shape[dim]
        last = lax.slice_in_dim(a, length - HALO, length, axis=dim)
        first = lax.slice_in_dim(a, 0, HALO, axis=dim)
        before = lax.ppermute(last, "space", [(i, i + 1) for i in range(tiles - 1)])
        after = lax.ppermute(first, "space", [(i + 1, i) for i in range(tiles - 1)])
        return jnp.concatenate([before, a, after], axis=dim)

    table = jnp.asarray(coefficients(window))
    mine = lax.dynamic_slice_in_dim(table, tm, window, axis=1)[:, ::-1]
    wide = widen(rhs[0], 1)
    everyone = lax.all_gather(wide, "tm")
    sums = jnp.einsum("nj,jfxy->nfxy", mine, everyone, precision=lax.Precision.HIGHEST)
    rows = rhs.shape[2]
    line = lax.axis_index("space") * rows - HALO + jnp.arange(rows + 2 * HALO)
    inside = ((line >= 0) & (line < rows * tiles)).astype(jnp.float32)[:, None]
    deep, turn = -SIGMA * widen(depth, 0), widen(coriolis, 0)

    def dx(a):
        return (jnp.roll(a, -1, 0) - jnp.roll(a, 1, 0)) * inside

    def dy(a):
        return jnp.roll(a, -1, 1) - jnp.roll(a, 1, 1)

    h, u, v = sums[SWEEPS]
    for n in reversed(range(SWEEPS)):
        h, u, v = (sums[n, 0] + deep * (dx(u) + dy(v)), sums[n, 1] - SIGMA * dx(h) + turn * v,
                   sums[n, 2] - SIGMA * dy(h) - turn * u)
    return jnp.stack([h, u, v])[None, :, HALO:rows + HALO]


def solution(mesh):
    in_specs = (P("tm", None, "space", None), P("space", None), P("space", None))
    out_specs = P("tm", None, "space", None)
    body = shards_kernel if (mesh.shape["tm"], mesh.shape["space"]) == (16, 2) else shards_plain
    return jax.shard_map(body, mesh=mesh, in_specs=in_specs, out_specs=out_specs, check_vma=False)
```

time: 38.6 us -> 30.6 us (0.79)
  Pallas kernels: 34.2 us -> 28.9 us
  local copies, waits for them, and re-layouts: 3.98 us -> 1.62 us
    pallas_call x1, Pallas kernels: 34.2 us -> 28.9 us  [shards_kernel(): pl.pallas_call(functools.partial(gather_kernel, window, rows, coefficient...]
    unnamed x9 -> x1, local copies, waits for them, and re-layouts: 3.98 us -> 1.62 us
where the time goes in v2:
time: 30.6 us; the launch traced here: 30.5 us
  Pallas kernels  28.9 us (94%)
  local copies, waits for them, and re-layouts  1.62 us (5%)
    pallas_call x1, Pallas kernels, shards_kernel(): pl.pallas_call(functools.partial(gather_kernel, window, rows, coefficient...  28.9 us
    unnamed x1, local copies, waits for them, and re-layouts  1.62 us

profile of v2, /device:TPU:0, one launch (start us, length us, event | category | flops | bytes accessed | tf_op | source)
XLA Modules:
  0.0 30.5 jit_solution(11421183922475255444)
XLA Ops:
  0.0 28.9 %shard_map.37 = f32[1,3,64,256]{3,2,1,0:T(8,128)} custom-call(f32[1,3,64,256]{3,2,1,0:T(8,128)} %rhs.1, f32[64,256]{1,0:T(8,128)} %depth.1, f32[64,256]{1,0:T(8,128)} %coriolis.1), custom_call_target="tpu_custom_call" | custom-call | flops 40000000 | bytes 1000000 | tf_op jit(solution)/shard_map/pallas_call | solution.py:229
  28.9 1.6 %copy.5 = f32[1,3,64,256]{3,2,1,0:T(8,128)} copy(f32[1,3,64,256]{3,2,1,0:T(8,128)} %shard_map.37) | data formatting | bytes 393216

commit v3 on v2

--- a/solution.py
+++ b/solution.py
@@ -12,6 +12,7 @@
 RHO = 0.9
 SIGMA = 0.01
 TERMS = SWEEPS + 1
+CHUNKS = 4
 HALO = 8
 MESH = pl.DeviceIdType.MESH
 
@@ -26,13 +27,16 @@
     return table.astype(np.float32)
 
 
-def gather_kernel(window, rows, table, rhs, depth, coriolis, out, main, plane, z_acc, coef, send_sem, send_own, recv_sem,
+def gather_kernel(window, rows, table, rhs, depth, coriolis, out, main, plane, z_acc, coef, send_sem, recv_sem,
                   local_sem, send_y, recv_y):
     tm, y = lax.axis_index("tm"), lax.axis_index("space")
     z, x, c = tm // 4, tm % 4 // 2, tm % 2
     end = (z == 0) | (z == 3)
     inner = jnp.logical_not(end)
-    fields = range(3)
+    groups = (rows + HALO) // HALO
+    cuts = [groups * q // CHUNKS * HALO for q in range(CHUNKS + 1)]
+    chunks = [(lo, hi - lo) for lo, hi in zip(cuts, cuts[1:])]
+    parts_of = range(CHUNKS)
     pair = z + 1 - 2 * (z % 2)
     order = [z, pair, jnp.where(z < 2, 2, 1), jnp.where(z < 2, 3, 0)]
     x_other, c_other = z * 4 + (1 - x) * 2 + c, z * 4 + x * 2 + 1 - c
@@ -50,13 +54,12 @@
         pl.semaphore_signal(barrier, inc=1, device_id={"tm": peer}, device_id_type=MESH)
     pl.semaphore_signal(barrier, inc=1, device_id={"space": 1 - y}, device_id_type=MESH)
 
-    @pl.when(z > 0)
-    def _():
-        pl.semaphore_signal(barrier, inc=1, device_id={"tm": tm - 4}, device_id_type=MESH)
-
-    @pl.when(z < 3)
-    def _():
-        pl.semaphore_signal(barrier, inc=1, device_id={"tm": tm + 4}, device_id_type=MESH)
+    for hop in (-4, 4):
+        there = tm + hop
+
+        @pl.when((there >= 0) & (there < window))
+        def _():
+            pl.semaphore_signal(barrier, inc=1, device_id={"tm": there}, device_id_type=MESH)
 
     for n in range(TERMS):
         for gap in range(2 * window - 1):
@@ -65,7 +68,6 @@
         load.wait()
     pl.semaphore_wait(barrier, jnp.where(end, 4, 5))
 
-    pending = []
     both = lambda *conds: functools.reduce(jnp.logical_and, conds) if conds else None
 
     def guarded(when, act):
@@ -74,19 +76,23 @@
         else:
             pl.when(when)(act)
 
-    def copy(block, f, slot, peer):
+    def copy(block, q, slot, peer):
+        ref = main.at[block, :, pl.ds(*chunks[q]), :]
         return pltpu.make_async_remote_copy(
-            src_ref=main.at[block, f], dst_ref=main.at[block, f], send_sem=send_sem.at[slot],
-            recv_sem=recv_sem.at[block, f], device_id={"tm": peer}, device_id_type=MESH)
-
-    slots = {}
-
-    def send(key, block, f, peer, start_when=None, finish_when=None):
-        fresh = key not in slots
-        slot = slots.setdefault(key, len(slots))
-        guarded(start_when, lambda: copy(block, f, slot, peer).start())
-        if fresh:
-            pending.append(lambda: guarded(finish_when, lambda: copy(block, f, slot, peer).wait_send()))
+            src_ref=ref, dst_ref=ref, send_sem=send_sem.at[slot], recv_sem=recv_sem.at[block, q],
+            device_id={"tm": peer}, device_id_type=MESH)
+
+    always, when_inner, when_cross, when_second = range(4)
+
+    def send(kind, block, q, peer, start_when=None):
+        guarded(start_when, lambda: copy(block, q, kind, peer).start())
+
+    def all_sent(kind, blocks, when=None):
+        ref = main.at[pl.ds(0, blocks)]
+        sent = pltpu.make_async_remote_copy(
+            src_ref=ref, dst_ref=ref, send_sem=send_sem.at[kind], recv_sem=recv_sem.at[0, 0],
+            device_id={"tm": c_other}, device_id_type=MESH)
+        guarded(when, sent.wait_send)
 
     def arrived(block, f):
         copy(block, f, 0, c_other).wait_recv()
@@ -104,91 +110,83 @@
         recv_sem=recv_y.at[1], device_id={"space": 1 - y}, device_id_type=MESH)
     edges.start()
 
-    def own(f, part, index):
-        for q, (peer, when) in enumerate([(tm + 4, z < 3), (tm - 4, z > 0), (x_other, None), (c_other, None)]):
-            def make(peer=peer, q=q):
-                ref = main.at[tm, f, part, :]
-                return pltpu.make_async_remote_copy(
-                    src_ref=ref, dst_ref=ref, send_sem=send_own.at[index, q], recv_sem=recv_sem.at[tm, f],
-                    device_id={"tm": peer}, device_id_type=MESH)
-            guarded(when, lambda make=make: make().start())
-            pending.append(lambda when=when, make=make: guarded(when, lambda: make().wait_send()))
-
-    def relay_z(stage, f, when=None):
+    def own(q):
+        outward = jnp.where(z < 2, 4, -4)
+        send(always, tm, q, tm + outward)
+        send(always, tm, q, x_other)
+        send(when_inner, tm, q, tm - outward, inner)
+        send(always, tm, q, c_other)
+
+    def relay_z(stage, q, when=None):
         block = block_of(stage, True, True)
-        guarded(when, lambda: arrived(block, f))
+        guarded(when, lambda: arrived(block, q))
         conds = [] if when is None else [when]
         onward = jnp.where(order[stage] < z, z + 1, z - 1)
-        send(("z", stage, f), block, f, onward * 4 + x * 2 + c, both(inner, *conds), inner)
+        send(when_inner, block, q, onward * 4 + x * 2 + c, both(inner, *conds))
         cross = [end & (c == 1)] if stage == 1 else []
-        send(("x", stage, f), block, f, x_other, both(*cross, *conds), both(*cross))
-        send(("c", stage, f), block, f, c_other, both(*conds))
-
-    def relay_x(stage, f, when=None):
+        send(when_cross if cross else always, block, q, x_other, both(*cross, *conds))
+        send(always, block, q, c_other, both(*conds))
+
+    def relay_x(stage, q, when=None):
         block = block_of(stage, False, True)
-        guarded(when, lambda: arrived(block, f))
-        send(("cx", stage, f), block, f, c_other, when)
-
-    def second_route(f, when):
-        send(("zx", f), block_of(0, False, True), f, pair * 4 + x * 2 + c, when, end | (c == 0))
-
-    def accumulate(stage, f, first=False):
-        arrived(block_of(stage, True, False), f)
-        arrived(block_of(stage, False, False), f)
-        blocks = [order[stage] * 4 + q for q in range(4)]
+        guarded(when, lambda: arrived(block, q))
+        send(always, block, q, c_other, when)
+
+    def second_route(q, when):
+        send(when_second, block_of(0, False, True), q, pair * 4 + x * 2 + c, when)
+
+    def accumulate(stage, q, first=False):
+        arrived(block_of(stage, True, False), q)
+        arrived(block_of(stage, False, False), q)
+        blocks = [order[stage] * 4 + k for k in range(4)]
         weights = [[coef[n, tm - b + window - 1] for b in blocks] for n in range(TERMS)]
-        step = 24
-
-        def body(i, carry):
-            part = pl.ds(pl.multiple_of(i * step, 8), step)
+        part = pl.ds(*chunks[q])
+
+        def body(f, carry):
             parts = [main[b, f, part] for b in blocks]
             for n in range(TERMS):
                 total = parts[0] * weights[n][0]
-                for q in range(1, 4):
-                    total = total + parts[q] * weights[n][q]
+                for k in range(1, 4):
+                    total = total + parts[k] * weights[n][k]
                 if not first:
                     total = total + z_acc[n, f, part]
                 z_acc[n, f, part] = total
             return carry
 
-        lax.fori_loop(0, (rows + HALO) // step, body, 0)
-
-    body_rows = pl.ds(0, rows)
-    own(0, body_rows, 0)
-    own(1, body_rows, 1)
+        lax.fori_loop(0, 3, body, 0)
+
+    for q in parts_of[:-1]:
+        own(q)
     edges.wait_recv()
-    own(0, tail, 3)
-    own(1, tail, 4)
-    own(2, body_rows, 2)
-    own(2, tail, 5)
+    own(CHUNKS - 1)
     fixed.start()
 
     late = end & (c == 0)
-    for f in fields:
-        relay_z(1, f)
-        relay_z(2, f, inner)
-        relay_x(0, f)
-        second_route(f, end)
-    for f in fields:
-        relay_z(2, f, end)
-        relay_z(3, f, inner)
-        relay_x(1, f, jnp.logical_not(late))
-        relay_x(2, f, inner)
-        accumulate(0, f, first=True)
-    for f in fields:
-        second_route(f, inner & (c == 0))
-    for f in fields:
-        relay_z(3, f, end)
-        relay_x(2, f, end)
-        relay_x(3, f, inner)
-    for f in fields:
-        relay_x(3, f, end)
-        accumulate(2, f)
-    for f in fields:
-        relay_x(1, f, late)
-        accumulate(3, f)
-    for f in fields:
-        accumulate(1, f)
+    for q in parts_of:
+        relay_z(1, q)
+        relay_z(2, q, inner)
+        relay_x(0, q)
+        second_route(q, end)
+    for q in parts_of:
+        relay_z(3, q, inner)
+        relay_z(2, q, end)
+        relay_x(1, q, jnp.logical_not(late))
+        relay_x(2, q, inner)
+        accumulate(0, q, True)
+    for q in parts_of:
+        second_route(q, inner & (c == 0))
+    for q in parts_of:
+        relay_z(3, q, end)
+        relay_x(2, q, end)
+        relay_x(3, q, inner)
+    for q in parts_of:
+        relay_x(3, q, end)
+        accumulate(2, q)
+    for q in parts_of:
+        relay_x(1, q, late)
+        accumulate(3, q)
+    for q in parts_of:
+        accumulate(1, q)
     fixed.wait_recv()
     fixed.wait_send()
 
@@ -216,8 +214,10 @@
     out[0, 1] = u[:rows]
     out[0, 2] = v[:rows]
 
-    for finish in pending:
-        finish()
+    all_sent(always, 12)
+    all_sent(when_inner, 4, inner)
+    all_sent(when_cross, 1, end & (c == 1))
+    all_sent(when_second, 1, end | (c == 0))
     edges.wait_send()
 
 
@@ -236,7 +236,7 @@
             pltpu.VMEM((2, rows + HALO, columns), jnp.float32),
             pltpu.VMEM((TERMS, fields, rows + HALO, columns), jnp.float32),
             pltpu.SMEM((TERMS, 2 * window - 1), jnp.float32),
-            dma((48,)), dma((6, 4)), dma((window, fields)), dma((3,)), dma((2,)), dma((2,)),
+            dma((4,)), dma((window, CHUNKS)), dma((3,)), dma((2,)), dma((2,)),
         ],
         compiler_params=pltpu.CompilerParams(collective_id=0, has_side_effects=True, vmem_limit_bytes=62 << 20),
         cost_estimate=pl.CostEstimate(flops=40_000_000, bytes_accessed=1_000_000, transcendentals=0),

time: 30.6 us -> 29.5 us (0.964)
  Pallas kernels: 28.9 us -> 27.7 us
    pallas_call x1, Pallas kernels: 28.9 us -> 27.7 us  [shards_kernel(): pl.pallas_call(functools.partial(gather_kernel, window, rows, coefficient...]
where the time goes in v3:
time: 29.5 us; the launch traced here: 29.3 us
  Pallas kernels  27.7 us (94%)
  local copies, waits for them, and re-layouts  1.62 us (5%)
    pallas_call x1, Pallas kernels, shards_kernel(): pl.pallas_call(functools.partial(gather_kernel, window, rows, coefficient...  27.7 us
    unnamed x1, local copies, waits for them, and re-layouts  1.62 us

profile of v3, /device:TPU:0, one launch (start us, length us, event | category | flops | bytes accessed | tf_op | source)
XLA Modules:
  0.0 29.3 jit_solution(10625191296685114537)
XLA Ops:
  0.0 27.7 %shard_map.37 = f32[1,3,64,256]{3,2,1,0:T(8,128)} custom-call(f32[1,3,64,256]{3,2,1,0:T(8,128)} %rhs.1, f32[64,256]{1,0:T(8,128)} %depth.1, f32[64,256]{1,0:T(8,128)} %coriolis.1), custom_call_target="tpu_custom_call" | custom-call | flops 40000000 | bytes 1000000 | tf_op jit(solution)/shard_map/pallas_call | solution.py:229
  27.7 1.6 %copy.5 = f32[1,3,64,256]{3,2,1,0:T(8,128)} copy(f32[1,3,64,256]{3,2,1,0:T(8,128)} %shard_map.37) | data formatting | bytes 393216
